TPU v7x, 128 devices: a whole 4x4x4 slice. The times are simulated.
128 devices in a mesh: tm: 32 (over x, z, core), state: 4 (over y).
Axes of the slice: x: 4, y: 4, z: 4, core: 2. Of those that a mesh axis runs over, the one named last changes fastest.
Arguments:
- dyn_cols: int32 [1024, 8, 3], P('tm', 'state'), may hold values from 0 to 7, as said below
- dyn_vals: bfloat16 [1024, 8, 64, 192], P('tm', 'state'), may hold values from -1 to 1
- obs_blocks: int32 [1024, 2], P('tm'), may hold values from 0 to 7
- obs_op: bfloat16 [1024, 64, 128], P('tm'), may hold values from -0.75 to 0.75
- obs_counts: int32 [1024], P('tm'), may hold values from 32 to 128, as said below
- obs_values: float32 [1024, 128], P('tm'), may hold values from -6 to 6
- gain: bfloat16 [1024, 512, 128], P('tm', 'state'), may hold values from -0.0078125 to 0.0078125
- sources: float32 [1024, 512], P('tm', 'state'), may hold values from -0.625 to 0.625
- prior: float32 [512], replicated, may hold values from -6 to 6
Outputs:
- filtered: float32 [1024, 512], P('tm', 'state')
Inputs may be any that keep to these rules, and one draw needn't show every extreme that they name: `dyn_cols`: for every step and block row i, the first entry is i itself and the 3 entries are distinct block columns. `obs_counts`: some step has all 128 observations present.
All inputs are finite; a program needn't handle non-finite values.
Results may differ from a plain program's by a relative error of at most 0.0003.
The roundings to bfloat16 on the way count: a program that leaves them out, or rounds other values in their place, can miss the bound.
Values may be sent and summed in bfloat16 or wider, within the bound.
A program may use at most 128 MiB of HBM per device.

v0:
```python
import jax
import jax.numpy as jnp
from jax import lax
from jax.sharding import PartitionSpec as P

NS = 512
BS = 64
KF = 3
OBS = 128
NB = 8
OB = 2
HIGHEST = lax.Precision.HIGHEST


def prefix(value, axis, join, neutral):
    count, mine = (lax.axis_size(axis), lax.axis_index(axis))
    pieces = jax.tree.map(lambda part: lax.all_gather(part, axis), value)
    so_far = jax.tree.map(
        lambda part, zero: jnp.full_like(part, 0) + jnp.asarray(zero, part.dtype), value, neutral
    )

    def step(position, so_far):
        longer = join(so_far, jax.tree.map(lambda part: part[position], pieces))
        return jax.tree.map(lambda new, old: jnp.where(position < mine, new, old), longer, so_far)

    return lax.fori_loop(0, count - 1, step, so_far)


def split_product(matrix, operand):
    leading = operand.astype(jnp.bfloat16)
    remainder = (operand - lax.optimization_barrier(leading).astype(jnp.float32)).astype(
        jnp.bfloat16
    )
    return jnp.dot(matrix, leading, preferred_element_type=jnp.float32) + jnp.dot(
        matrix, remainder, preferred_element_type=jnp.float32
    )


def body(dyn_cols, dyn_vals, obs_blocks, obs_op, obs_counts, obs_values, gain, sources, prior):
    step_count = dyn_vals.shape[0]
    local_blocks = dyn_vals.shape[1]
    local_rows = local_blocks * BS
    state_index = lax.axis_index("state")
    onehot = (dyn_cols[..., None] == jnp.arange(NB)).astype(jnp.bfloat16)
    blocks = dyn_vals.reshape(step_count, local_blocks, BS, KF, BS)
    forward = jnp.einsum("tikc,tiakb->tiacb", onehot, blocks, preferred_element_type=jnp.float32)
    forward = forward.reshape(step_count, local_blocks, BS, NS)
    forward_narrow = forward.astype(jnp.bfloat16)
    owned = state_index * local_blocks + jnp.arange(local_blocks)
    select = obs_blocks[:, :, None] == owned[None, None, :]
    selected = jnp.einsum(
        "tos,tsbn->tobn",
        select.astype(jnp.bfloat16),
        forward_narrow,
        preferred_element_type=jnp.float32,
    ).astype(jnp.bfloat16)
    operator_blocks = obs_op.reshape(step_count, BS, OB, BS)
    image_part = jnp.einsum(
        "tboa,tobn->toan", operator_blocks, selected, preferred_element_type=jnp.float32
    )
    image_part = image_part.reshape(step_count, OBS, NS)
    source_sel = jnp.einsum(
        "tos,tsb->tob",
        select.astype(jnp.float32),
        sources.reshape(step_count, local_blocks, BS),
        precision=HIGHEST,
    )
    source_part = jnp.einsum(
        "tboa,tob->toa", operator_blocks.astype(jnp.float32), source_sel, precision=HIGHEST
    )
    source_part = source_part.reshape(step_count, OBS)
    image_sum, source_sum = (
        lax.psum(image_part.astype(jnp.bfloat16), "state").astype(jnp.float32),
        lax.psum(source_part.astype(jnp.bfloat16), "state").astype(jnp.float32),
    )
    active = jnp.arange(OBS)[None, :] < obs_counts[:, None]
    masked = jnp.where(
        active[:, :, None], image_sum.astype(jnp.bfloat16), jnp.zeros((), jnp.bfloat16)
    )
    source_image = lax.optimization_barrier(source_sum.astype(jnp.bfloat16)).astype(jnp.float32)
    innovation = jnp.where(active, obs_values - source_image, 0.0)
    correction = jnp.einsum("tro,ton->trn", gain, masked, preferred_element_type=jnp.float32)
    element = (forward.reshape(step_count, local_rows, NS) - correction).astype(jnp.bfloat16)
    offset = sources + jnp.einsum(
        "tro,to->tr", gain.astype(jnp.float32), innovation, precision=HIGHEST
    )
    full_elements = lax.all_gather(element, "state", axis=1, tiled=True)
    full_offsets = lax.all_gather(offset, "state", axis=1, tiled=True)
    start_cols = (
        jnp.arange(NS)[:, None] == (state_index * local_rows + jnp.arange(local_rows))[None, :]
    ).astype(jnp.float32)

    def compose(carry, inputs):
        product, vector = carry
        matrix, shift_term = inputs
        product = split_product(matrix, product)
        vector = split_product(matrix, vector) + shift_term
        return ((product, vector), None)

    (column_product, span_offset), _ = lax.scan(
        compose, (start_cols, jnp.zeros((NS,), jnp.float32)), (full_elements, full_offsets)
    )
    span_matrix = lax.all_gather(column_product, "state", axis=1, tiled=True)

    def combine(earlier, later):
        return (
            jnp.dot(later[0], earlier[0], precision=HIGHEST),
            jnp.dot(later[0], earlier[1], precision=HIGHEST) + later[1],
        )

    identity = (jnp.eye(NS, dtype=jnp.float32), jnp.zeros((NS,), jnp.float32))
    before = prefix((span_matrix, span_offset), "tm", combine, identity)
    entry = jnp.dot(before[0], prior, precision=HIGHEST) + before[1]

    def sweep(current, inputs):
        matrix, shift_term = inputs
        new_mean = split_product(matrix, current) + shift_term
        return (new_mean, lax.dynamic_slice_in_dim(new_mean, state_index * local_rows, local_rows))

    _, filtered = lax.scan(sweep, entry, (full_elements, full_offsets))
    return filtered


def solution(mesh):
    return jax.shard_map(
        body,
        mesh=mesh,
        in_specs=(
            P("tm", "state", None),
            P("tm", "state", None, None),
            P("tm", None),
            P("tm", None, None),
            P("tm"),
            P("tm", None),
            P("tm", "state", None),
            P("tm", "state"),
            P(),
        ),
        out_specs=P("tm", "state"),
        check_vma=False,
    )
```

profile of v0, /device:TPU:1, one launch (start us, length us, event | category | flops | bytes accessed | tf_op | source)
XLA Modules:
  0.0 967.0 jit_solution(8072769552737119339)
XLA Ops:
  6.5 4.6 copy.27
  11.1 7.2 copy.28
  18.4 10.6 %fusion.58 = (bf16[32,2,64,8,64]{4,3,2,1,0:T(8,128)(2,1)}, f32[32,2,64,8,64]{4,3,2,1,0:T(8,128)}) fusion(bf16[32,2,64,3,64]{4,3,2,1,0:T(4,128)(2,1)} %copy.28, s32[32,2,3]{2,1,0:T(2,128)S(1)} %copy.26), kind=kOutput, calls=%fused_computation.79 | convolution fusion | flops 14681600 | bytes 14156544 | tf_op jit(solution)/shard_map/tikc,tiakb->tiacb/dot_general | solution.py:46
  29.0 11.9 %convert_element_type.81 = bf16[32,2,64,512]{3,2,1,0:T(8,128)(2,1)} reshape(bf16[32,2,64,8,64]{4,3,2,1,0:T(8,128)(2,1)} %get-tuple-element.329) | data formatting | bytes 8388608 | tf_op jit(solution)/shard_map/convert_element_type | solution.py:48
  41.4 8.8 convolution_convert_fusion
  50.2 3.2 fusion.39
  53.4 6.4 copy.33
  59.9 14.6 %reshape_reshape.3 = f32[32,128,512]{2,1,0:T(8,128)} reshape(f32[32,2,64,8,64]{4,3,2,1,0:T(8,128)} %get-tuple-element.330) | data formatting | bytes 16777216 | tf_op jit(solution)/shard_map/reshape;reshape | solution.py:83
  74.6 9.0 copy.34
  83.7 72.4 %all-reduce.2.cloned.1.call-done = bf16[32,128,512]{1,2,0:T(8,128)(2,1)} async-done(((bf16[32,128,512]{1,2,0:T(8,128)(2,1)}), bf16[32,128,512]{1,2,0:T(8,128)(2,1)}) %all-reduce.2.cloned.1.call-update) | async-done | bytes 4194320 | tf_op jit(solution)/shard_map/psum | solution.py:73
  156.1 7.9 fusion.30
  165.5 6.6 psum.15
  173.9 9.6 all_gather.22
  183.5 138.3 %all-gather.7.cloned.1.call-done = bf16[32,512,512]{1,2,0:T(8,128)(2,1)} async-done(((bf16[32,128,512]{1,2,0:T(8,128)(2,1)}), bf16[32,512,512]{1,2,0:T(8,128)(2,1)}) %all-gather.7.cloned.1.call-update) | async-done | bytes 16777232 | tf_op jit(solution)/shard_map/all_gather | solution.py:87
  321.8 22.6 %copy.35 = bf16[32,512,512]{2,1,0:T(8,128)(2,1)} copy(bf16[32,512,512]{1,2,0:T(8,128)(2,1)} %all-gather.7.cloned.1.call-done) | data formatting | bytes 33554432
  344.4 173.2 %while.47 = (s32[]{:T(128)}, f32[512,128]{1,0:T(8,128)S(1)}, f32[512]{0:T(512)S(1)}, bf16[32,512,512]{2,1,0:T(8,128)(2,1)}, f32[32,512]{1,0:T(8,128)S(1)}) while((s32[]{:T(128)}, f32[512,128]{1,0:T(8,128)S(1)}, f32[512]{0:T(512)S(1)}, bf16[32,512,512]{2,1,0:T(8,128)(2,1)}, f32[32,512]{1,0:T(8,128)S(1)}) %tuple.85), condition=%wide.region_3.4_spmd.clone.clone, body=%wide.region_2.3_spmd.clone.sunk.clone | while | flops 135597568 | bytes 4357196 | solution.py:100
  518.4 26.3 %all-gather.9.cloned.1.call-done = f32[512,512]{1,0:T(8,128)} async-done(((f32[512,128]{1,0:T(8,128)}), f32[512,512]{1,0:T(8,128)}) %all-gather.9.cloned.1.call-update) | async-done | bytes 1048592 | tf_op jit(solution)/shard_map/all_gather | solution.py:103
  544.9 25.7 %all-gather.2 = f32[32,1,512]{2,1,0:T(1,128)S(1)} all-gather(f32[1,1,512]{2,1,0:T(1,128)S(1)} %bitcast.166), channel_id=3, replica_groups=mesh['tm'=32,'state'=4] {'tm'}, dimensions={0}, use_global_device_ids=true | all-gather | bytes 67584 | tf_op jit(solution)/shard_map/all_gather | solution.py:17
  570.6 92.8 %all-gather.11.cloned.1.call-done = f32[16384,512]{1,0:T(8,128)} async-done(((f32[512,512]{1,0:T(8,128)}), f32[16384,512]{1,0:T(8,128)}) %all-gather.11.cloned.1.call-update) | async-done | bytes 33554448 | tf_op jit(solution)/shard_map/all_gather | solution.py:17
  663.4 168.3 %while.48 = (s32[]{:T(128)}, f32[512,512]{1,0:T(8,128)S(1)}, f32[512]{0:T(512)S(1)}, s32[]{:T(128)}, f32[32,512,512]{2,1,0:T(8,128)}, /*index=5*/f32[32,512]{1,0:T(8,128)S(1)}) while((s32[]{:T(128)}, f32[512,512]{1,0:T(8,128)S(1)}, f32[512]{0:T(512)S(1)}, s32[]{:T(128)}, f32[32,512,512]{2,1,0:T(8,128)}, ...), condition=%wide.region_5.6_spmd.clone.clone, body=%wide.region_4.5_spmd.clone.sunk.clone | while | flops 1614022656 | bytes 7361631 | solution.py:26
  663.4 2.2 fusion.138
  665.7 3.1 convolution_select_fusion.3
  671.2 3.1 convolution_select_fusion.3
  676.6 3.1 convolution_select_fusion.3
  682.0 3.1 convolution_select_fusion.3
  687.4 3.1 convolution_select_fusion.3
  690.6 2.2 fusion.138
  692.9 3.1 convolution_select_fusion.3
  696.0 2.2 fusion.138
  698.3 3.1 convolution_select_fusion.3
  701.4 2.2 fusion.138
  703.7 3.1 convolution_select_fusion.3
  709.2 3.1 convolution_select_fusion.3
  712.3 2.2 fusion.138
  714.6 3.1 convolution_select_fusion.3
  717.7 2.2 fusion.138
  720.0 3.1 convolution_select_fusion.3
  725.5 3.1 convolution_select_fusion.3
  730.9 3.1 convolution_select_fusion.3
  736.3 3.1 convolution_select_fusion.3
  739.4 2.2 fusion.138
  741.7 3.1 convolution_select_fusion.3
  744.9 2.2 fusion.138
  747.2 3.1 convolution_select_fusion.3
  750.3 2.2 fusion.138
  752.6 3.1 convolution_select_fusion.3
  755.7 2.2 fusion.138
  758.0 3.1 convolution_select_fusion.3
  761.1 2.2 fusion.138
  763.5 3.1 convolution_select_fusion.3
  766.6 2.2 fusion.138
  768.9 3.1 convolution_select_fusion.3
  774.3 3.1 convolution_select_fusion.3
  779.8 3.1 convolution_select_fusion.3
  785.2 3.1 convolution_select_fusion.3
  790.6 3.1 convolution_select_fusion.3
  796.0 3.1 convolution_select_fusion.3
  801.5 3.1 convolution_select_fusion.3
  806.9 3.1 convolution_select_fusion.3
  812.3 3.1 convolution_select_fusion.3
  817.8 3.1 convolution_select_fusion.3
  823.2 3.1 convolution_select_fusion.3
  828.6 3.1 convolution_select_fusion.3
  832.7 127.8 %while.46 = (s32[]{:T(128)}, f32[512]{0:T(512)S(1)}, f32[32,128]{1,0:T(8,128)}, bf16[32,512,512]{2,1,0:T(8,128)(2,1)}, f32[32,512]{1,0:T(8,128)S(1)}, /*index=5*/s32[]{:T(128)}) while((s32[]{:T(128)}, f32[512]{0:T(512)S(1)}, f32[32,128]{1,0:T(8,128)}, bf16[32,512,512]{2,1,0:T(8,128)(2,1)}, f32[32,512]{1,0:T(8,128)S(1)}, ...), condition=%wide.region_7.8_spmd.clone, body=%wide.region_6.7_spmd.sunk.clone | while | flops 1051650 | bytes 1081425 | solution.py:120
  (895 shorter events, 349.4 us)
Async XLA Ops:
  6.5 149.5 %copy-start = (bf16[32,128,128]{2,1,0:T(8,128)(2,1)S(1)}, bf16[32,128,128]{2,1,0:T(8,128)(2,1)}, u32[]{:S(2)}) copy-start(bf16[32,128,128]{2,1,0:T(8,128)(2,1)} %param.21) | copy-start | bytes 3145732
  6.5 11.7 %copy-start.5 = (s32[32,2,3]{0,1,2:T(2,128)S(1)}, s32[32,2,3]{0,1,2:T(2,128)}, u32[]{:S(2)}) copy-start(s32[32,2,3]{0,1,2:T(2,128)} %param.15) | copy-start | bytes 2308
  6.5 149.5 %all-reduce.2.cloned.1.call-start = ((), (), s32[]{:S(2)}) async-start(), calls=%async_computation | async-start | bytes 8388608 | tf_op jit(solution)/shard_map/psum | solution.py:73
  29.0 11.9 %copy-start.8 = (s32[32,2]{0,1:T(2,128)S(1)}, s32[32,2]{0,1:T(2,128)}, u32[]{:S(2)}) copy-start(s32[32,2]{0,1:T(2,128)} %param.17) | copy-start | bytes 772
  29.0 12.0 %copy-start.2 = (bf16[32,64,128]{2,1,0:T(8,128)(2,1)S(1)}, bf16[32,64,128]{2,1,0:T(8,128)(2,1)}, u32[]{:S(2)}) copy-start(bf16[32,64,128]{2,1,0:T(8,128)(2,1)} %param.18) | copy-start | bytes 1572868
  59.9 261.9 %all-gather.7.cloned.1.call-start = ((), (), s32[]{:S(2)}) async-start(), calls=%async_computation.1 | async-start | bytes 20971520 | tf_op jit(solution)/shard_map/all_gather | solution.py:87
  74.6 9.0 copy-start.7
  83.7 80.3 %copy-start.3 = (f32[32,128]{1,0:T(8,128)S(1)}, f32[32,128]{1,0:T(8,128)}, u32[]{:S(2)}) copy-start(f32[32,128]{1,0:T(8,128)} %param.22) | copy-start | bytes 49156
  83.7 88.4 %copy-start.4 = (f32[32,128]{1,0:T(8,128)S(1)}, f32[32,128]{1,0:T(8,128)}, u32[]{:S(2)}) copy-start(f32[32,128]{1,0:T(8,128)} %param.20) | copy-start | bytes 49156
  164.0 380.8 %all-gather.9.cloned.1.call-start = ((), (), s32[]{:S(2)}) async-start(), calls=%async_computation.2 | async-start | bytes 1310720 | tf_op jit(solution)/shard_map/all_gather | solution.py:103
  517.7 0.7 copy-start.1
  518.4 145.0 %all-gather.11.cloned.1.call-start = ((), (), s32[]{:S(2)}) async-start(), calls=%async_computation.3 | async-start | bytes 34603008 | tf_op jit(solution)/shard_map/all_gather | solution.py:17
  663.4 168.3 %copy-start.6 = (f32[512]{0:T(512)S(1)}, f32[512]{0:T(512)}, u32[]{:S(2)}) copy-start(f32[512]{0:T(512)} %param.23) | copy-start | bytes 6148
Sparse Core Ops, SparseCore 0:
  60.0 96.0 all-reduce.1
  164.1 157.6 all-gather.6
  518.5 26.1 all-gather.8
  547.1 116.2 all-gather.10
where the time goes:
time: 981 us; the launch traced here: 967 us
  matrix products  448 us (46%)
  waiting for transfers between devices  330 us (34%)
  local copies, waits for them, and re-layouts  126 us (13%)
  blocking collectives  41.9 us (4%)
  between operations  13.3 us (1%)
    all_gather x1, waiting for transfers between devices, body(): full_elements = lax.all_gather(element, 'state', axis=1, tiled=True)  138 us
    dot_general x96, matrix products, split_product(): jnp.dot(matrix, leading, preferred_element_type=jnp.float32)  126 us
    dot_general x96, matrix products, split_product(): jnp.dot(matrix, remainder, preferred_element_type=jnp.float32)  125 us
    dot_general x31, matrix products, combine(): jnp.dot(later[0], earlier[0], precision=HIGHEST)  95.1 us
    all_gather x1, waiting for transfers between devices, prefix(): pieces = jax.tree.map(lambda part: lax.all_gather(part, axis), value)  92.8 us
    psum x1, waiting for transfers between devices, body(): lax.psum(image_part.astype(jnp.bfloat16), 'state').astype(jnp.float32)  72.4 us
    dot_general x31, matrix products, combine(): jnp.dot(later[0], earlier[1], precision=HIGHEST) + later[1]  68.3 us
    dynamic_update_slice x32, local copies, waits for them, and re-layouts, body(): _, filtered = lax.scan(sweep, entry, (full_elements, full_offsets))  41.3 us
  transfers between devices with their start and end apart: 4, of which 4 were waited for; matrix products, arithmetic and copies ran while one was open for 3% of the time, Pallas kernels for 0%

commit v1 on v0

--- a/solution.py
+++ b/solution.py
@@ -100,7 +100,19 @@
     (column_product, span_offset), _ = lax.scan(
         compose, (start_cols, jnp.zeros((NS,), jnp.float32)), (full_elements, full_offsets)
     )
-    span_matrix = lax.all_gather(column_product, "state", axis=1, tiled=True)
+    size, index, rows = (lax.axis_size("state"), lax.axis_index("state"), column_product.shape[1])
+    right = [(i, (i + 1) % size) for i in range(size)]
+    result = jnp.zeros(
+        (*column_product.shape[:1], size * rows, *column_product.shape[1 + 1 :]),
+        column_product.dtype,
+    )
+    held = column_product
+    for hop in range(size):
+        source = (index - hop) % size
+        result = lax.dynamic_update_slice_in_dim(result, held, source * rows, axis=1)
+        if hop < size - 1:
+            held = lax.ppermute(held, "state", right)
+    span_matrix = result
 
     def combine(earlier, later):
         return (

time: 981 us -> 975 us (level)
  waiting for transfers between devices: 330 us -> 319 us
    all_gather x1 -> x0, waiting for transfers between devices: 26.3 us -> none  [body(): span_matrix = lax.all_gather(column_product, 'state', axis=1, tiled=True)]
    ppermute x0 -> x3, waiting for transfers between devices: none -> 20.1 us  [body(): held = lax.ppermute(held, 'state', right)]
  transfers between devices with their start and end apart: 4 -> 6, of which waited for: 4 -> 6; matrix products, arithmetic and copies ran while one was open for 3% -> 3% of each run, Pallas kernels for 0% -> 0%
where the time goes in v1:
time: 975 us; the launch traced here: 960 us
  matrix products  448 us (46%)
  waiting for transfers between devices  319 us (33%)
  local copies, waits for them, and re-layouts  127 us (13%)
  blocking collectives  45.2 us (5%)
  between operations  13.3 us (1%)
    all_gather x1, waiting for transfers between devices, body(): full_elements = lax.all_gather(element, 'state', axis=1, tiled=True)  138 us
    dot_general x96, matrix products, split_product(): jnp.dot(matrix, leading, preferred_element_type=jnp.float32)  126 us
    dot_general x96, matrix products, split_product(): jnp.dot(matrix, remainder, preferred_element_type=jnp.float32)  125 us
    dot_general x31, matrix products, combine(): jnp.dot(later[0], earlier[0], precision=HIGHEST)  95.1 us
    all_gather x1, waiting for transfers between devices, prefix(): pieces = jax.tree.map(lambda part: lax.all_gather(part, axis), value)  88.4 us
    psum x1, waiting for transfers between devices, body(): lax.psum(image_part.astype(jnp.bfloat16), 'state').astype(jnp.float32)  72.4 us
    dot_general x31, matrix products, combine(): jnp.dot(later[0], earlier[1], precision=HIGHEST) + later[1]  68.3 us
    dynamic_update_slice x32, local copies, waits for them, and re-layouts, body(): _, filtered = lax.scan(sweep, entry, (full_elements, full_offsets))  41.3 us
  transfers between devices with their start and end apart: 6, of which 6 were waited for; matrix products, arithmetic and copies ran while one was open for 3% of the time, Pallas kernels for 0%

profile of v1, /device:TPU:1, one launch (start us, length us, event | category | flops | bytes accessed | tf_op | source)
XLA Modules:
  0.0 960.3 jit_solution(1751004534365124944)
XLA Ops:
  6.5 4.6 copy.27
  11.1 7.2 copy.28
  18.4 10.6 %fusion.58 = (bf16[32,2,64,8,64]{4,3,2,1,0:T(8,128)(2,1)}, f32[32,2,64,8,64]{4,3,2,1,0:T(8,128)}) fusion(bf16[32,2,64,3,64]{4,3,2,1,0:T(4,128)(2,1)} %copy.28, s32[32,2,3]{2,1,0:T(2,128)S(1)} %copy.26), kind=kOutput, calls=%fused_computation.83 | convolution fusion | flops 14681600 | bytes 14156544 | tf_op jit(solution)/shard_map/tikc,tiakb->tiacb/dot_general | solution.py:46
  29.0 11.9 %convert_element_type.81 = bf16[32,2,64,512]{3,2,1,0:T(8,128)(2,1)} reshape(bf16[32,2,64,8,64]{4,3,2,1,0:T(8,128)(2,1)} %get-tuple-element.329) | data formatting | bytes 8388608 | tf_op jit(solution)/shard_map/convert_element_type | solution.py:48
  41.4 8.8 convolution_convert_fusion
  50.2 3.2 fusion.39
  53.4 6.4 copy.33
  59.9 14.6 %reshape_reshape.3 = f32[32,128,512]{2,1,0:T(8,128)} reshape(f32[32,2,64,8,64]{4,3,2,1,0:T(8,128)} %get-tuple-element.330) | data formatting | bytes 16777216 | tf_op jit(solution)/shard_map/reshape;reshape | solution.py:83
  74.6 9.0 copy.34
  83.7 72.4 %all-reduce.2.cloned.1.call-done = bf16[32,128,512]{1,2,0:T(8,128)(2,1)} async-done(((bf16[32,128,512]{1,2,0:T(8,128)(2,1)}), bf16[32,128,512]{1,2,0:T(8,128)(2,1)}) %all-reduce.2.cloned.1.call-update) | async-done | bytes 4194320 | tf_op jit(solution)/shard_map/psum | solution.py:73
  156.1 7.9 fusion.30
  165.5 6.6 psum.15
  173.9 9.6 all_gather.28
  183.5 138.3 %all-gather.5.cloned.1.call-done = bf16[32,512,512]{1,2,0:T(8,128)(2,1)} async-done(((bf16[32,128,512]{1,2,0:T(8,128)(2,1)}), bf16[32,512,512]{1,2,0:T(8,128)(2,1)}) %all-gather.5.cloned.1.call-update) | async-done | bytes 16777232 | tf_op jit(solution)/shard_map/all_gather | solution.py:87
  321.8 22.6 %copy.35 = bf16[32,512,512]{2,1,0:T(8,128)(2,1)} copy(bf16[32,512,512]{1,2,0:T(8,128)(2,1)} %all-gather.5.cloned.1.call-done) | data formatting | bytes 33554432
  344.4 173.2 %while.47 = (s32[]{:T(128)}, f32[512,128]{1,0:T(8,128)S(1)}, f32[512]{0:T(512)S(1)}, bf16[32,512,512]{2,1,0:T(8,128)(2,1)}, f32[32,512]{1,0:T(8,128)S(1)}) while((s32[]{:T(128)}, f32[512,128]{1,0:T(8,128)S(1)}, f32[512]{0:T(512)S(1)}, bf16[32,512,512]{2,1,0:T(8,128)(2,1)}, f32[32,512]{1,0:T(8,128)S(1)}) %tuple.85), condition=%wide.region_3.4_spmd.clone.clone, body=%wide.region_2.3_spmd.clone.sunk.clone | while | flops 135597568 | bytes 4357196 | solution.py:100
  517.7 7.5 collective-permute-done
  525.4 6.3 collective-permute-done.1
  531.7 6.4 collective-permute-done.2
  539.3 29.0 %all-gather.1 = f32[32,1,512]{2,1,0:T(1,128)S(1)} all-gather(f32[1,1,512]{2,1,0:T(1,128)S(1)} %bitcast.172), channel_id=2, replica_groups=mesh['tm'=32,'state'=4] {'tm'}, dimensions={0}, use_global_device_ids=true | all-gather | bytes 67584 | tf_op jit(solution)/shard_map/all_gather | solution.py:17
  568.3 88.4 %all-gather.7.cloned.1.call-done = f32[32,512,512]{2,1,0:T(8,128)} async-done(((f32[1,512,512]{2,1,0:T(8,128)}), f32[32,512,512]{2,1,0:T(8,128)}) %all-gather.7.cloned.1.call-update) | async-done | bytes 33554448 | tf_op jit(solution)/shard_map/all_gather | solution.py:17
  656.6 168.3 %while.48 = (s32[]{:T(128)}, f32[512,512]{1,0:T(8,128)S(1)}, f32[512]{0:T(512)S(1)}, s32[]{:T(128)}, f32[32,512,512]{2,1,0:T(8,128)}, /*index=5*/f32[32,512]{1,0:T(8,128)S(1)}) while((s32[]{:T(128)}, f32[512,512]{1,0:T(8,128)S(1)}, f32[512]{0:T(512)S(1)}, s32[]{:T(128)}, f32[32,512,512]{2,1,0:T(8,128)}, ...), condition=%wide.region_5.6_spmd.clone.clone, body=%wide.region_4.5_spmd.clone.sunk.clone | while | flops 1614022656 | bytes 7361631 | solution.py:26
  656.6 2.2 fusion.138
  659.0 3.1 convolution_select_fusion.3
  662.1 2.2 fusion.138
  664.4 3.1 convolution_select_fusion.3
  667.5 2.2 fusion.138
  669.8 3.1 convolution_select_fusion.3
  672.9 2.2 fusion.138
  675.3 3.1 convolution_select_fusion.3
  678.4 2.2 fusion.138
  680.7 3.1 convolution_select_fusion.3
  683.8 2.2 fusion.138
  686.1 3.1 convolution_select_fusion.3
  689.2 2.2 fusion.138
  691.6 3.1 convolution_select_fusion.3
  694.7 2.2 fusion.138
  697.0 3.1 convolution_select_fusion.3
  700.1 2.2 fusion.138
  702.4 3.1 convolution_select_fusion.3
  705.5 2.2 fusion.138
  707.8 3.1 convolution_select_fusion.3
  713.3 3.1 convolution_select_fusion.3
  718.7 3.1 convolution_select_fusion.3
  724.1 3.1 convolution_select_fusion.3
  729.6 3.1 convolution_select_fusion.3
  735.0 3.1 convolution_select_fusion.3
  740.4 3.1 convolution_select_fusion.3
  745.9 3.1 convolution_select_fusion.3
  751.3 3.1 convolution_select_fusion.3
  756.7 3.1 convolution_select_fusion.3
  762.1 3.1 convolution_select_fusion.3
  767.6 3.1 convolution_select_fusion.3
  773.0 3.1 convolution_select_fusion.3
  778.4 3.1 convolution_select_fusion.3
  783.9 3.1 convolution_select_fusion.3
  789.3 3.1 convolution_select_fusion.3
  794.7 3.1 convolution_select_fusion.3
  800.2 3.1 convolution_select_fusion.3
  805.6 3.1 convolution_select_fusion.3
  811.0 3.1 convolution_select_fusion.3
  816.4 3.1 convolution_select_fusion.3
  821.9 3.1 convolution_select_fusion.3
  826.0 127.8 %while.46 = (s32[]{:T(128)}, f32[512]{0:T(512)S(1)}, f32[32,128]{1,0:T(8,128)}, bf16[32,512,512]{2,1,0:T(8,128)(2,1)}, f32[32,512]{1,0:T(8,128)S(1)}, /*index=5*/s32[]{:T(128)}) while((s32[]{:T(128)}, f32[512]{0:T(512)S(1)}, f32[32,128]{1,0:T(8,128)}, bf16[32,512,512]{2,1,0:T(8,128)(2,1)}, f32[32,512]{1,0:T(8,128)S(1)}, ...), condition=%wide.region_7.8_spmd.clone, body=%wide.region_6.7_spmd.sunk.clone | while | flops 1051650 | bytes 1081425 | solution.py:132
  (903 shorter events, 354.4 us)
Async XLA Ops:
  6.5 149.5 %copy-start = (bf16[32,128,128]{2,1,0:T(8,128)(2,1)S(1)}, bf16[32,128,128]{2,1,0:T(8,128)(2,1)}, u32[]{:S(2)}) copy-start(bf16[32,128,128]{2,1,0:T(8,128)(2,1)} %param.21) | copy-start | bytes 3145732
  6.5 11.7 %copy-start.5 = (s32[32,2,3]{0,1,2:T(2,128)S(1)}, s32[32,2,3]{0,1,2:T(2,128)}, u32[]{:S(2)}) copy-start(s32[32,2,3]{0,1,2:T(2,128)} %param.15) | copy-start | bytes 2308
  6.5 149.5 %all-reduce.2.cloned.1.call-start = ((), (), s32[]{:S(2)}) async-start(), calls=%async_computation | async-start | bytes 8388608 | tf_op jit(solution)/shard_map/psum | solution.py:73
  29.0 11.9 %copy-start.8 = (s32[32,2]{0,1:T(2,128)S(1)}, s32[32,2]{0,1:T(2,128)}, u32[]{:S(2)}) copy-start(s32[32,2]{0,1:T(2,128)} %param.17) | copy-start | bytes 772
  29.0 12.0 %copy-start.2 = (bf16[32,64,128]{2,1,0:T(8,128)(2,1)S(1)}, bf16[32,64,128]{2,1,0:T(8,128)(2,1)}, u32[]{:S(2)}) copy-start(bf16[32,64,128]{2,1,0:T(8,128)(2,1)} %param.18) | copy-start | bytes 1572868
  59.9 261.9 %all-gather.5.cloned.1.call-start = ((), (), s32[]{:S(2)}) async-start(), calls=%async_computation.1 | async-start | bytes 20971520 | tf_op jit(solution)/shard_map/all_gather | solution.py:87
  74.6 9.0 copy-start.7
  83.7 80.3 %copy-start.3 = (f32[32,128]{1,0:T(8,128)S(1)}, f32[32,128]{1,0:T(8,128)}, u32[]{:S(2)}) copy-start(f32[32,128]{1,0:T(8,128)} %param.22) | copy-start | bytes 49156
  83.7 88.4 %copy-start.4 = (f32[32,128]{1,0:T(8,128)S(1)}, f32[32,128]{1,0:T(8,128)}, u32[]{:S(2)}) copy-start(f32[32,128]{1,0:T(8,128)} %param.20) | copy-start | bytes 49156
  164.0 492.7 %all-gather.7.cloned.1.call-start = ((), (), s32[]{:S(2)}) async-start(), calls=%async_computation.2 | async-start | bytes 34603008 | tf_op jit(solution)/shard_map/all_gather | solution.py:17
  517.7 7.5 collective-permute-start
  525.2 6.4 collective-permute-start.1
  531.6 6.4 collective-permute-start.2
  538.1 1.0 copy-start.1
  656.6 168.3 %copy-start.6 = (f32[512]{0:T(512)S(1)}, f32[512]{0:T(512)}, u32[]{:S(2)}) copy-start(f32[512]{0:T(512)} %param.23) | copy-start | bytes 6148
Sparse Core Ops, SparseCore 0:
  60.0 96.0 all-reduce.1
  164.1 157.6 all-gather.4
  539.2 117.3 all-gather.6
